TPU v7x, 512 devices: a whole 4x4x16 slice. The times are simulated.
512 devices in a mesh: dp: 16 (over x, y), expert: 32 (over z, core).
Axes of the slice: x: 4, y: 4, z: 16, core: 2. Of those that a mesh axis runs over, the one named last changes fastest.
Arguments:
- cotangent: bfloat16 [65536, 5120], P(('dp', 'expert')), may hold values from -6 to 6
- route_weights: float32 [65536, 6], P(('dp', 'expert')), may hold values from 0.05 to 1
- token_experts: int32 [65536, 6], P(('dp', 'expert')), may hold values from 0 to 159, as said below
- saved_hidden: bfloat16 [16, 32, 32, 16, 1536], P('dp', 'expert'), may hold values from -6 to 6
- previous_right: bfloat16 [32, 1536, 128], P('expert', 'dp'), may hold values from -8 to 8
Outputs:
- left_factor: float32 [32, 5120, 128], P('expert', 'dp')
- right_factor: float32 [32, 1536, 128], P('expert', 'dp')
Inputs may be any that keep to these rules, and one draw needn't show every extreme that they name: `token_experts`: each token names 6 different experts. On one device at most 16 tokens name any one of the experts 0 to 31, and in every draw one of these experts is named by exactly 16 tokens on every device.
All inputs are finite; a program needn't handle non-finite values.
Results may differ from a plain program's by a relative error of at most 0.0049.
Values may be sent and summed in bfloat16 or wider, within the bound.
A program may use at most 64 MiB of HBM per device.

v0:
```python
import math

import jax
import jax.numpy as jnp
from jax import lax
from jax.sharding import PartitionSpec as P

EPSILON = 1e-06


def cholesky_pass(block):
    gram = jnp.dot(
        block.T, block, precision=lax.Precision.HIGHEST, preferred_element_type=jnp.float32
    )
    lower = jnp.linalg.cholesky(gram)
    orthogonal = lax.linalg.triangular_solve(
        lower, block, left_side=False, lower=True, transpose_a=True
    )
    return (orthogonal, lower.T)


def orthonormal(block):
    first, upper_one = cholesky_pass(block)
    second, upper_two = cholesky_pass(first)
    return (
        second,
        jnp.dot(
            upper_two,
            upper_one,
            precision=lax.Precision.HIGHEST,
            preferred_element_type=jnp.float32,
        ),
    )


def local(cotangent, route_weights, token_experts, saved_hidden, previous_right):
    window = lax.axis_size("expert")
    shards = lax.axis_size("dp")
    position = lax.axis_index("dp")
    token_count = cotangent.shape[0]
    model_width = cotangent.shape[1]
    capacity = saved_hidden.shape[3]
    hidden_width = saved_hidden.shape[4]
    contract_rows = (((0,), (0,)), ((), ()))
    expert_range = jnp.arange(window, dtype=jnp.int32)
    matches = token_experts[:, :, None] == expert_range[None, None, :]
    routed = jnp.any(matches, axis=1).astype(jnp.int32)
    weight_sum = jnp.sum(jnp.where(matches, route_weights[:, :, None], 0.0), axis=1)
    slots = jnp.cumsum(routed, axis=0) - routed
    chosen = (routed[:, :, None] == 1) & (
        slots[:, :, None] == jnp.arange(capacity, dtype=jnp.int32)[None, None, :]
    )
    token_range = jnp.arange(token_count, dtype=jnp.int32)
    source_row = jnp.sum(jnp.where(chosen, token_range[:, None, None], 0), axis=0)
    slot_weight = jnp.sum(jnp.where(chosen, weight_sum[:, :, None], 0.0), axis=0)
    picked = jnp.take(cotangent, source_row.reshape(-1), axis=0).reshape(
        window, capacity, model_width
    )
    outgoing = (picked * slot_weight[:, :, None]).astype(jnp.bfloat16)
    arrived = lax.all_to_all(outgoing, "expert", split_axis=0, concat_axis=0, tiled=True).reshape(
        window * capacity, model_width
    )
    hidden_rows = saved_hidden.reshape(window * capacity, hidden_width)
    right_whole = lax.all_gather(previous_right[0], "dp", axis=0, tiled=True)
    projected = jnp.dot(hidden_rows, right_whole, preferred_element_type=jnp.float32).astype(
        jnp.bfloat16
    )
    own_rows = model_width // shards
    gathered_left_terms = lax.dot_general(
        arrived, projected, contract_rows, preferred_element_type=jnp.float32
    )
    left_sum = lax.psum(gathered_left_terms, "dp")
    complete_basis_matrix, triangle = orthonormal(left_sum)
    basis = lax.dynamic_slice_in_dim(complete_basis_matrix, position * own_rows, own_rows, 0)
    rotated_factor = jnp.dot(
        arrived, complete_basis_matrix.astype(jnp.bfloat16), preferred_element_type=jnp.float32
    ).astype(jnp.bfloat16)
    right_own = lax.psum_scatter(
        lax.dot_general(
            hidden_rows, rotated_factor, contract_rows, preferred_element_type=jnp.float32
        ),
        "dp",
        scatter_dimension=0,
        tiled=True,
    )
    column_sums = lax.psum(jnp.sum(right_own * right_own, axis=0), "dp")
    right_out = right_own * (math.sqrt(hidden_width) / jnp.sqrt(column_sums + EPSILON))
    left_out = basis * math.sqrt(model_width)
    return (left_out[None], right_out[None])


def solution(mesh):
    in_specs = (
        P(("dp", "expert"), None),
        P(("dp", "expert"), None),
        P(("dp", "expert"), None),
        P("dp", "expert", None, None, None),
        P("expert", "dp", None),
    )
    out_specs = (P("expert", "dp", None), P("expert", "dp", None))
    return jax.shard_map(local, mesh=mesh, in_specs=in_specs, out_specs=out_specs, check_vma=False)
```

profile of v0, /device:TPU:32, one launch (start us, length us, event | category | flops | bytes accessed | tf_op | source)
XLA Modules:
  0.0 621.0 jit_solution(2072789280997162327)
XLA Ops:
  7.2 0.0 copy-start
  7.2 0.8 fusion.11
  8.0 0.1 copy.25
  8.2 0.2 reduce_window_sum.11
  8.3 0.1 copy.27
  8.4 0.1 copy.26
  8.5 0.6 select_reduce_fusion.1
  9.1 0.1 reshape.85
  9.3 0.7 select_reduce_fusion.2
  10.0 0.1 select_reduce_fusion
  10.1 12.0 %gather_fusion = bf16[512,5120]{1,0:T(8,128)(2,1)} fusion(bf16[128,5120]{1,0:T(8,128)(2,1)} %param.8, s32[1024]{0:T(1024)S(1)} %pad_clamp_fusion), kind=kCustom, calls=%fused_computation | custom fusion | bytes 10487808 | tf_op jit(solution)/shard_map/jit(_take)/gather | solution.py:56
  22.1 7.9 %multiply_convert_fusion = bf16[32,16,5120]{2,1,0:T(8,128)(2,1)} fusion(f32[32,16]{1,0:T(8,128)S(1)} %select_reduce_fusion, bf16[32,16,5120]{2,1,0:T(8,128)(2,1)} %bitcast.49, pred[32,16]{1,0:T(8,128)(4,1)S(1)} %compare_and_fusion), kind=kLoop, calls=%fused_computation.1 | loop fusion | flops 10485760 | bytes 10488320 | tf_op jit(solution)/shard_map/convert_element_type | solution.py:59
  30.0 15.5 %all-to-all-start = ((bf16[32,16,5120]{2,1,0:T(8,128)(2,1)}), bf16[32,16,5120]{2,1,0:T(8,128)(2,1)}, u32[]{:S(2)}, u32[]{:S(2)}) async-start(bf16[32,16,5120]{2,1,0:T(8,128)(2,1)} %multiply_convert_fusion), calls=%async_computation | async-start | bytes 10485760 | tf_op jit(solution)/shard_map/all_to_all | solution.py:60
  45.5 0.0 all-reduce.2.cloned.1.call-start
  45.6 0.0 copy-done.2
  45.6 24.2 %all-gather = bf16[1,1536,128]{2,1,0:T(8,128)(2,1)S(1)} all-gather(bf16[1,96,128]{2,1,0:T(8,128)(2,1)S(1)} %copy-done.2), channel_id=2, replica_groups=mesh['dp'=16,'expert'=32] {'dp'}, dimensions={1}, use_global_device_ids=true | all-gather | bytes 417792 | tf_op jit(solution)/shard_map/all_gather | solution.py:64
  69.8 210.9 %all-to-all-done = bf16[32,16,5120]{2,1,0:T(8,128)(2,1)} async-done(((bf16[32,16,5120]{2,1,0:T(8,128)(2,1)}), bf16[32,16,5120]{2,1,0:T(8,128)(2,1)}, u32[]{:S(2)}, u32[]{:S(2)}) %all-to-all-start) | async-done | bytes 5242912 | tf_op jit(solution)/shard_map/all_to_all | solution.py:60
  280.7 0.0 copy-done
  280.7 6.8 %fusion.5 = f32[5120,128]{1,0:T(8,128)} fusion(bf16[512,5120]{1,0:T(8,128)(2,1)} %bitcast.2, bf16[512,1536]{1,0:T(8,128)(2,1)S(1)} %bitcast.47, bf16[1,1536,128]{2,1,0:T(8,128)(2,1)S(1)} %all-gather), kind=kOutput, calls=%fused_computation.9 | convolution fusion | flops 872480768 | bytes 9830400 | tf_op jit(solution)/shard_map/dot_general | solution.py:69
  287.5 0.0 all-reduce.2.cloned.1.call-update
  287.5 0.3 reduce-scatter.4.cloned.1.call-start
  287.8 115.7 %all-reduce.2.cloned.1.call-done = f32[5120,128]{1,0:T(8,128)} async-done(((f32[5120,128]{1,0:T(8,128)}), f32[5120,128]{1,0:T(8,128)}) %all-reduce.2.cloned.1.call-update) | async-done | bytes 2621456 | tf_op jit(solution)/shard_map/psum | solution.py:72
  403.5 6.8 %fusion.20 = f32[128,128]{1,0:T(8,128)S(1)} fusion(f32[5120,128]{1,0:T(8,128)} %all-reduce.2.cloned.1.call-done), kind=kOutput, calls=%fused_computation.45 | convolution fusion | flops 1006632960 | bytes 2686976 | tf_op jit(solution)/shard_map/dot_general | solution.py:12
  410.3 0.1 copy.28
  410.4 11.7 %cholesky.44 = f32[128,128]{1,0:T(8,128)S(1)} custom-call(f32[128,128]{1,0:T(8,128)S(1)} %fusion.17), custom_call_target="Cholesky" | custom-call | tf_op jit(solution)/shard_map/jit(cholesky)/cholesky | solution.py:15
  422.2 0.6 compare_reduce_fusion.1
  422.8 0.7 fusion.12
  423.5 9.8 %custom-call.6 = f32[1,128,128]{1,2,0:T(8,128)S(1)} custom-call(f32[1,128,128]{2,1,0:T(8,128)S(1)} %fusion.12), custom_call_target="InvertDiagBlocksLowerTriangular" | custom-call | tf_op jit(solution)/shard_map/triangular_solve/custom-call.0 | solution.py:16
  433.3 14.2 %convolution_bitcast_fusion.1 = f32[5120,128]{0,1:T(8,128)S(1)} fusion(f32[5120,128]{1,0:T(8,128)} %all-reduce.2.cloned.1.call-done, f32[1,128,128]{1,2,0:T(8,128)S(1)} %custom-call.6), kind=kOutput, calls=%fused_computation.3 | convolution fusion | flops 1006632960 | bytes 5308416 | tf_op jit(solution)/shard_map/triangular_solve/dot.4 | solution.py:16
  447.5 1.6 copy-done.1
  449.0 2.2 fusion.21
  451.2 0.1 copy.29
  451.4 11.7 %cholesky.55 = f32[128,128]{1,0:T(8,128)S(1)} custom-call(f32[128,128]{1,0:T(8,128)S(1)} %fusion.15), custom_call_target="Cholesky" | custom-call | tf_op jit(solution)/shard_map/jit(cholesky)/cholesky | solution.py:15
  463.1 0.6 compare_reduce_fusion
  463.8 0.7 fusion.13
  464.4 9.8 %custom-call.7 = f32[1,128,128]{1,2,0:T(8,128)S(1)} custom-call(f32[1,128,128]{2,1,0:T(8,128)S(1)} %fusion.13), custom_call_target="InvertDiagBlocksLowerTriangular" | custom-call | tf_op jit(solution)/shard_map/triangular_solve/custom-call.0 | solution.py:16
  474.2 5.6 convolution_bitcast_fusion
  479.8 5.5 convolution_bitcast_fusion.2
  485.3 1.1 copy.32
  486.5 0.0 reduce-scatter.4.cloned.1.call-update
  486.5 1.1 multiply_bitcast_fusion
  487.6 0.8 copy.30
  488.4 85.7 %reduce-scatter.4.cloned.1.call-done = f32[96,128]{1,0:T(8,128)} async-done(((f32[1536,128]{1,0:T(8,128)}), f32[96,128]{1,0:T(8,128)}) %reduce-scatter.4.cloned.1.call-update) | async-done | bytes 49168
  574.0 0.9 copy.33
  574.9 0.1 multiply_reduce_fusion
  575.1 38.1 %psum.15 = f32[128]{0:T(128)S(1)} all-reduce(f32[128]{0:T(128)S(1)} %multiply_reduce_fusion), channel_id=1, replica_groups=mesh['dp'=16,'expert'=32] {'dp'}, use_global_device_ids=true, to_apply=%region_10.13 | all-reduce | flops 128 | bytes 1024 | tf_op jit(solution)/shard_map/psum | solution.py:86
  613.2 0.1 multiply_bitcast_fusion.1
  613.3 0.7 copy.31
  (12 shorter events, 0.2 us)
Async XLA Ops:
  7.2 273.5 %copy-start = (bf16[1,1,32,16,1536]{4,3,2,1,0:T(8,128)(2,1)S(1)}, bf16[1,1,32,16,1536]{4,3,2,1,0:T(8,128)(2,1)}, u32[]{:S(2)}) copy-start(bf16[1,1,32,16,1536]{4,3,2,1,0:T(8,128)(2,1)} %param.11) | copy-start | bytes 4718596
  30.0 15.6 %copy-start.2 = (bf16[1,96,128]{2,1,0:T(8,128)(2,1)S(1)}, bf16[1,96,128]{2,1,0:T(8,128)(2,1)}, u32[]{:S(2)}) copy-start(bf16[1,96,128]{2,1,0:T(8,128)(2,1)} %param.12) | copy-start | bytes 73732
  30.0 250.7 %all-to-all-start = ((bf16[32,16,5120]{2,1,0:T(8,128)(2,1)}), bf16[32,16,5120]{2,1,0:T(8,128)(2,1)}, u32[]{:S(2)}, u32[]{:S(2)}) async-start(bf16[32,16,5120]{2,1,0:T(8,128)(2,1)} %multiply_convert_fusion), calls=%async_computation | async-start | bytes 10485760 | tf_op jit(solution)/shard_map/all_to_all | solution.py:60
  45.5 358.0 %all-reduce.2.cloned.1.call-start = ((), (), s32[]{:S(2)}) async-start(), calls=%async_computation.2 | async-start | bytes 5242880 | tf_op jit(solution)/shard_map/psum | solution.py:72
  287.5 286.5 %reduce-scatter.4.cloned.1.call-start = ((), (), s32[]{:S(2)}) async-start(), calls=%async_computation.3 | async-start | bytes 835584
  447.5 1.6 copy-start.1
Sparse Core Ops, SparseCore 0:
  287.6 115.8 all-reduce.1
  486.6 87.3 reduce-scatter.3
where the time goes:
time: 625 us; the launch traced here: 621 us
  waiting for transfers between devices  412 us (66%)
  blocking collectives  62.3 us (10%)
  other arithmetic  57.4 us (9%)
  matrix products  41.1 us (7%)
  local copies, waits for them, and re-layouts  17.6 us (3%)
  starting transfers between devices  15.9 us (3%)
  between operations  14.4 us (2%)
    all_to_all x1, waiting for transfers between devices, local(): lax.all_to_all(outgoing, 'expert', split_axis=0, concat_axis=0, tiled=True)  211 us
    psum x1, waiting for transfers between devices, local(): left_sum = lax.psum(gathered_left_terms, 'dp')  116 us
    unnamed x3, waiting for transfers between devices  85.7 us
    psum x1, blocking collectives, local(): column_sums = lax.psum(jnp.sum(right_own * right_own, axis=0), 'dp')  38.1 us
    another operation x6, other arithmetic, cholesky_pass(): lower = jnp.linalg.cholesky(gram)  24.8 us
    all_gather x1, blocking collectives, local(): right_whole = lax.all_gather(previous_right[0], 'dp', axis=0, tiled=True)  24.2 us
    another operation x4, other arithmetic, cholesky_pass(): lax.linalg.triangular_solve(lower, block, left_side=False, lower=True, tr...  20.9 us
    another operation x2, matrix products, cholesky_pass(): lax.linalg.triangular_solve(lower, block, left_side=False, lower=True, tr...  19.8 us
  transfers between devices with their start and end apart: 3, of which 3 were waited for; matrix products, arithmetic and copies ran while one was open for 0% of the time, Pallas kernels for 0%

commit v1 on v0

v1 whole, which is shorter than its diff:
```python
import functools
import math

import jax
import jax.numpy as jnp
from jax import lax
from jax.experimental import pallas as pl
from jax.experimental.pallas import tpu as pltpu
from jax.sharding import PartitionSpec as P

EPSILON = 1e-06
MESH = pl.DeviceIdType.MESH
F32 = jnp.float32
BF16 = jnp.bfloat16
HIGHEST = lax.Precision.HIGHEST


class Sizes:
    def __init__(self, n_dp, n_expert, tokens, width, capacity, hidden, rank, chunks):
        self.n_dp, self.n_expert = n_dp, n_expert
        self.n_z = n_expert // 2
        assert self.n_z == n_dp
        self.ny = int(round(math.sqrt(n_dp)))
        self.tokens, self.width, self.capacity = tokens, width, capacity
        self.hidden, self.rank, self.chunks = hidden, rank, chunks
        self.rows = n_expert * capacity
        self.wide = width // chunks
        self.piece = self.wide // self.n_z
        self.pair = 2 * capacity
        self.own_left = width // n_dp
        self.own_right = hidden // n_dp
        self.half = self.n_z // 2


def inverse_factor(gram_ref, inverse_ref, size):
    lane = lax.broadcasted_iota(jnp.int32, (size, size), 1)
    sub = lax.broadcasted_iota(jnp.int32, (size, size), 0)
    inverse_ref[...] = jnp.where(lane == sub, 1.0, 0.0).astype(F32)

    def step(j, carry):
        row = gram_ref[pl.ds(j, 1), :]
        inv_row = inverse_ref[pl.ds(j, 1), :]
        first = lax.broadcasted_iota(jnp.int32, (1, size), 1)
        pivot = jnp.sum(jnp.where(first == j, row, 0.0), axis=1, keepdims=True)
        gram = gram_ref[...]
        column = jnp.sum(jnp.where(lane == j, gram, 0.0), axis=1, keepdims=True)
        factor = jnp.where(sub[:, :1] > j, column / pivot, 0.0)
        gram_ref[...] = gram - factor * row
        inverse_ref[...] = inverse_ref[...] - factor * inv_row
        return carry

    lax.fori_loop(0, size, step, 0)
    pivots = jnp.sum(jnp.where(lane == sub, gram_ref[...], 0.0), axis=1, keepdims=True)
    inverse_ref[...] = inverse_ref[...] * lax.rsqrt(pivots)


def kernel(
    m,
    cot, weights, experts, hidden, previous,
    left_out, right_out,
    key_s, wsum_s, pick_s, scale_s,
    out_s, arr_s, prev_s, proj_s, turn_s, projected_s,
    part_s, from_left, from_right, own_s, full_s,
    gram_s, inverse_s, acc_s, rot_s, back_s, left_s, terms_s, landed_s, square_s, squares_s,
    row_send, row_recv, prev_sem, turn_sem, proj_sem,
    sum_right, sum_left, gat_right, gat_left, back_sem, left_sem, terms_sem, square_sem,
):
    i = lax.axis_index("dp")
    e = lax.axis_index("expert")
    z = lax.div(e, 2)
    c = lax.rem(e, 2)
    me = i * 2 + c
    K = m.chunks
    diagonal = i == z
    right_e = lax.rem(z + 1, m.n_z) * 2 + c
    left_e = lax.rem(z + m.n_z - 1, m.n_z) * 2 + c

    def peer(j):
        j = lax.rem(j * 11, 2 * m.n_dp)
        x = lax.rem(lax.div(i, m.ny) + lax.div(j, 2 * m.ny), m.ny)
        y = lax.rem(lax.rem(i, m.ny) + lax.rem(lax.div(j, 2), m.ny), m.ny)
        core = lax.rem(c + lax.rem(j, 2), 2)
        return x * m.ny + y, core

    def remote(src, dst, send, recv, to):
        return pltpu.make_async_remote_copy(
            src_ref=src, dst_ref=dst, send_sem=send, recv_sem=recv, device_id=to, device_id_type=MESH
        )

    def wait_bytes(ref, sem):
        pltpu.make_async_copy(ref, ref, sem).wait()

    barrier = pltpu.get_barrier_semaphore()

    def greet(to):
        pl.semaphore_signal(barrier, inc=1, device_id=to, device_id_type=MESH)

    @pl.loop(1, 2 * m.n_dp)
    def _(j):
        a, core = peer(j)
        greet((a, z * 2 + core))

    @pl.loop(1, m.n_z)
    def _(j):
        greet((i, lax.rem(z + j, m.n_z) * 2 + c))

    @pl.loop(0, m.n_dp)
    def _(j):
        @pl.when(jnp.logical_not(jnp.logical_and(diagonal, j == i)))
        def _():
            greet((j, i * 2 + c))

        @pl.when(jnp.logical_not(jnp.logical_and(diagonal, j == z)))
        def _():
            greet((z, j * 2 + c))

    ids = experts[...]
    values = weights[...]
    square = (m.tokens, m.tokens)
    lane = lax.broadcasted_iota(jnp.int32, square, 1)
    sub = lax.broadcasted_iota(jnp.int32, square, 0)
    wsum = jnp.zeros(square, F32)
    routed = jnp.zeros(square, F32)
    for t in range(ids.shape[1]):
        hit = ids[:, t : t + 1] == lane
        wsum = wsum + jnp.where(hit, values[:, t : t + 1], 0.0)
        routed = jnp.where(hit, 1.0, routed)
    wsum_s[...] = wsum.T[: m.n_expert]
    routed_t = routed.T[: m.n_expert]
    before = jnp.where(sub < lane, 1.0, 0.0).astype(BF16)
    slots = jnp.dot(routed_t.astype(BF16), before, preferred_element_type=F32)
    key_s[...] = jnp.where(routed_t > 0.0, slots, -1.0)

    @pl.loop(0, m.n_expert)
    def _(x):
        slot = lax.broadcasted_iota(jnp.int32, (m.capacity, m.tokens), 0).astype(F32)
        hit = key_s[pl.ds(x, 1), :] == slot
        rows = pl.ds(pl.multiple_of(x * m.capacity, m.capacity), m.capacity)
        pick_s[rows, :] = jnp.where(hit, 1.0, 0.0).astype(BF16)
        weight = jnp.sum(jnp.where(hit, wsum_s[pl.ds(x, 1), :], 0.0), axis=1, keepdims=True)
        scale_s[rows, :] = jnp.broadcast_to(weight, (m.capacity, m.tokens))

    def scale_rows(k):
        @pl.loop(0, m.wide // 128)
        def _(n):
            inside = pl.ds(pl.multiple_of(n * 128, 128), 128)
            whole = pl.ds(pl.multiple_of(k * m.wide + n * 128, 128), 128)
            picked = jnp.dot(pick_s[...], cot[:, whole], preferred_element_type=F32)
            out_s[k, :, inside] = (picked * scale_s[...]).astype(BF16)

    def rows_of(index, count):
        return pl.ds(pl.multiple_of(index * count, count), count)

    mine = rows_of(me, m.capacity)

    def send_rows(k):
        @pl.loop(1, 2 * m.n_dp)
        def _(j):
            a, core = peer(j)
            remote(
                out_s.at[k, rows_of(a * 2 + core, m.capacity)], arr_s.at[k, mine],
                row_send.at[k], row_recv.at[k], (a, z * 2 + core),
            ).start()

        arr_s[k, mine, :] = out_s[k, mine, :]

    scale_rows(0)
    pl.semaphore_wait(
        barrier, 2 * m.n_dp - 1 + m.n_z - 1 + 2 * m.n_dp - 2 * diagonal.astype(jnp.int32)
    )

    @pl.loop(1, m.n_dp)
    def _(j):
        remote(
            previous, prev_s.at[rows_of(i, m.own_right)],
            prev_sem.at[0], prev_sem.at[1], (lax.rem(i + j, m.n_dp), e),
        ).start()

    prev_s[rows_of(i, m.own_right), :] = previous[...]
    send_rows(0)
    others = (m.n_dp - 1) * m.own_right
    wait_bytes(prev_s.at[pl.ds(0, others)], prev_sem.at[1])

    proj_s[...] = jnp.dot(hidden[...], prev_s[...], preferred_element_type=F32).astype(BF16)

    @pl.loop(1, m.n_z)
    def _(j):
        to = lax.rem(z + j, m.n_z)
        remote(
            proj_s.at[rows_of(to, m.pair)], turn_s.at[rows_of(z, m.pair)],
            turn_sem.at[0], turn_sem.at[1], (i, to * 2 + c),
        ).start()

    turn_s[rows_of(z, m.pair), :] = proj_s[rows_of(z, m.pair), :]
    scale_rows(1)
    send_rows(1)
    most = pl.ds(0, (m.n_z - 1) * m.pair)
    wait_bytes(turn_s.at[most], turn_sem.at[1])

    @pl.loop(1, m.n_dp)
    def _(j):
        to = lax.rem(i + j, m.n_dp)
        remote(
            turn_s.at[rows_of(to, m.pair)], projected_s.at[rows_of(i, m.pair)],
            proj_sem.at[0], proj_sem.at[1], (to, e),
        ).start()

    projected_s[rows_of(i, m.pair), :] = turn_s[rows_of(i, m.pair), :]
    for k in range(2, K):
        scale_rows(k)
        send_rows(k)
    wait_bytes(projected_s.at[most], proj_sem.at[1])

    def piece_of(index):
        return rows_of(index, m.piece)

    def shifted(shift):
        return lax.rem(z + shift + 2 * m.n_z, m.n_z)

    def left_terms(k):
        @pl.loop(0, m.wide // 128)
        def _(n):
            inside = pl.ds(pl.multiple_of(n * 128, 128), 128)
            turned = lax.dot_general(
                projected_s[...], arr_s[k, :, inside], (((0,), (0,)), ((), ())),
                preferred_element_type=F32,
            )
            part_s[k, inside, :] = turned.T

    half = m.half

    def sum_copy(k, s, rightward, src):
        if rightward:
            return remote(src, from_left.at[k, s], sum_right.at[0, k, s], sum_right.at[1, k, s], (i, right_e))
        return remote(src, from_right.at[k, s], sum_left.at[0, k, s], sum_left.at[1, k, s], (i, left_e))

    def sum_first(k):
        sum_copy(k, 0, True, part_s.at[k, piece_of(shifted(half))]).start()
        sum_copy(k, 0, False, part_s.at[k, piece_of(shifted(1 - half))]).start()

    def sum_step(k, s):
        wait_bytes(from_left.at[k, s - 1], sum_right.at[1, k, s - 1])
        from_left[k, s - 1] = from_left[k, s - 1] + part_s[k, piece_of(shifted(half - s)), :]
        sum_copy(k, s, True, from_left.at[k, s - 1]).start()

        @pl.when(s < half - 1)
        def _():
            wait_bytes(from_right.at[k, s - 1], sum_left.at[1, k, s - 1])
            from_right[k, s - 1] = from_right[k, s - 1] + part_s[k, piece_of(shifted(1 - half + s)), :]
            sum_copy(k, s, False, from_right.at[k, s - 1]).start()

    def sum_last(k):
        wait_bytes(from_left.at[k, half - 1], sum_right.at[1, k, half - 1])
        wait_bytes(from_right.at[k, half - 2], sum_left.at[1, k, half - 2])
        total = part_s[k, piece_of(z), :] + from_left[k, half - 1] + from_right[k, half - 2]
        own_s[k] = total
        full_s[k, piece_of(z), :] = total.astype(BF16)

    def gather_copy(k, s, rightward):
        if rightward:
            block = full_s.at[k, piece_of(shifted(-s))]
            return remote(block, block, gat_right.at[0, k, s], gat_right.at[1, k, s], (i, right_e))
        block = full_s.at[k, piece_of(shifted(s))]
        return remote(block, block, gat_left.at[0, k, s], gat_left.at[1, k, s], (i, left_e))

    def gather_first(k):
        gather_copy(k, 0, True).start()
        gather_copy(k, 0, False).start()

    def gather_step(k, s):
        wait_bytes(full_s.at[k, piece_of(shifted(-s))], gat_right.at[1, k, s - 1])
        gather_copy(k, s, True).start()

        @pl.when(s < half - 1)
        def _():
            wait_bytes(full_s.at[k, piece_of(shifted(s))], gat_left.at[1, k, s - 1])
            gather_copy(k, s, False).start()

    def gather_last(k):
        wait_bytes(full_s.at[k, piece_of(shifted(-half))], gat_right.at[1, k, half - 1])
        wait_bytes(full_s.at[k, piece_of(shifted(half - 1))], gat_left.at[1, k, half - 2])

    gram_s[...] = jnp.zeros_like(gram_s)
    acc_s[...] = jnp.zeros_like(acc_s)

    def use_chunk(k):
        whole = full_s[k]
        gram_s[...] += lax.dot_general(
            whole, whole, (((0,), (0,)), ((), ())), preferred_element_type=F32
        )
        acc_s[...] += jnp.dot(arr_s[k], whole, preferred_element_type=F32)

    all_rows = pl.ds(0, (2 * m.n_dp - 1) * m.capacity)
    for k in range(K):
        wait_bytes(arr_s.at[k, all_rows], row_recv.at[k])
        left_terms(k)
        sum_first(k)
        if k > 0:
            gather_first(k - 1)

        @pl.loop(1, half)
        def _(s):
            sum_step(k, s)
            if k > 0:
                gather_step(k - 1, s)

        sum_last(k)
        if k > 0:
            gather_last(k - 1)
            use_chunk(k - 1)
    gather_first(K - 1)

    @pl.loop(1, half)
    def _(s):
        gather_step(K - 1, s)

    gather_last(K - 1)
    use_chunk(K - 1)

    inverse_factor(gram_s, inverse_s, m.rank)
    upper_inverse = inverse_s[...].T

    rot_s[...] = jnp.dot(
        acc_s[...], upper_inverse, precision=HIGHEST, preferred_element_type=F32
    ).astype(BF16)

    @pl.loop(0, m.n_dp)
    def _(j):
        to = lax.rem(i + j, m.n_dp)

        @pl.when(jnp.logical_not(jnp.logical_and(diagonal, to == i)))
        def _():
            remote(
                rot_s.at[rows_of(to, m.pair)], back_s.at[rows_of(z, m.pair)],
                back_sem.at[0], back_sem.at[1], (to, i * 2 + c),
            ).start()

    for k in range(K):
        left_s[k] = math.sqrt(m.width) * jnp.dot(
            own_s[k], upper_inverse, precision=HIGHEST, preferred_element_type=F32
        )

    def left_place(k):
        index = k * m.n_z + z
        return lax.div(index, K), rows_of(lax.rem(index, K), m.piece)

    def left_here(k):
        return jnp.logical_and(diagonal, left_place(k)[0] == i)

    for k in range(K):
        to, place = left_place(k)

        @pl.when(left_here(k))
        def _():
            left_out[place, :] = left_s[k]

        @pl.when(jnp.logical_not(left_here(k)))
        def _():
            remote(
                left_s.at[k], left_out.at[place], left_sem.at[0, k], left_sem.at[1, lax.rem(k * m.n_z + z, K)],
                (to, i * 2 + c),
            ).start()

    @pl.when(diagonal)
    def _():
        back_s[rows_of(z, m.pair), :] = rot_s[rows_of(i, m.pair), :]
        wait_bytes(back_s.at[most], back_sem.at[1])
        wait_bytes(rot_s.at[most], back_sem.at[0])

    @pl.when(jnp.logical_not(diagonal))
    def _():
        wait_bytes(back_s, back_sem.at[1])
        wait_bytes(rot_s, back_sem.at[0])

    @pl.loop(0, m.hidden // 128)
    def _(n):
        inside = pl.ds(pl.multiple_of(n * 128, 128), 128)
        turned = lax.dot_general(
            back_s[...], hidden[:, inside], (((0,), (0,)), ((), ())), preferred_element_type=F32
        )
        terms_s[inside, :] = turned.T

    @pl.loop(1, m.n_dp)
    def _(j):
        to = lax.rem(i + j, m.n_dp)
        remote(
            terms_s.at[rows_of(to, m.own_right)], landed_s.at[rows_of(i, m.own_right)],
            terms_sem.at[0], terms_sem.at[1], (to, e),
        ).start()

    landed_s[rows_of(i, m.own_right), :] = terms_s[rows_of(i, m.own_right), :]
    wait_bytes(landed_s.at[pl.ds(0, others)], terms_sem.at[1])
    right = landed_s[0 : m.own_right, :]
    for n in range(1, m.n_dp):
        right = right + landed_s[n * m.own_right : (n + 1) * m.own_right, :]
    square_s[...] = jnp.broadcast_to(jnp.sum(right * right, axis=0, keepdims=True), square_s.shape)

    @pl.loop(1, m.n_dp)
    def _(j):
        to = lax.rem(i + j, m.n_dp)
        remote(
            square_s, squares_s.at[rows_of(i, 8)], square_sem.at[0], square_sem.at[1], (to, e)
        ).start()

    squares_s[rows_of(i, 8), :] = square_s[...]
    wait_bytes(squares_s.at[pl.ds(0, (m.n_dp - 1) * 8)], square_sem.at[1])
    total = squares_s[0:1, :]
    for n in range(1, m.n_dp):
        total = total + squares_s[n * 8 : n * 8 + 1, :]
    right_out[...] = right * (math.sqrt(m.hidden) / jnp.sqrt(total + EPSILON))

    for k in range(K):
        wait_bytes(out_s.at[k, all_rows], row_send.at[k])

        @pl.loop(0, half)
        def _(s):
            wait_bytes(from_left.at[k, s], sum_right.at[0, k, s])
            wait_bytes(full_s.at[k, piece_of(0)], gat_right.at[0, k, s])

            @pl.when(s < half - 1)
            def _():
                wait_bytes(from_right.at[k, s], sum_left.at[0, k, s])
                wait_bytes(full_s.at[k, piece_of(0)], gat_left.at[0, k, s])

        @pl.when(jnp.logical_not(left_here(k)))
        def _():
            wait_bytes(left_s.at[k], left_sem.at[0, k])

        index = i * K + k
        source = lax.rem(index, m.n_z)

        @pl.when(jnp.logical_not(jnp.logical_and(diagonal, source == z)))
        def _():
            wait_bytes(left_s.at[k], left_sem.at[1, k])

    wait_bytes(prev_s.at[pl.ds(0, others)], prev_sem.at[0])
    wait_bytes(turn_s.at[most], turn_sem.at[0])
    wait_bytes(projected_s.at[most], proj_sem.at[0])
    wait_bytes(landed_s.at[pl.ds(0, others)], terms_sem.at[0])
    wait_bytes(squares_s.at[pl.ds(0, (m.n_dp - 1) * 8)], square_sem.at[0])


def local(chunks, cotangent, route_weights, token_experts, saved_hidden, previous_right):
    n_dp, n_expert = lax.axis_size("dp"), lax.axis_size("expert")
    tokens, width = cotangent.shape
    capacity, hidden = saved_hidden.shape[3:]
    rank = previous_right.shape[2]
    m = Sizes(n_dp, n_expert, tokens, width, capacity, hidden, rank, chunks)
    K, half = m.chunks, m.half
    vmem = pl.BlockSpec(memory_space=pltpu.VMEM)
    dma = pltpu.SemaphoreType.DMA
    left, right = pl.pallas_call(
        functools.partial(kernel, m),
        out_shape=(
            jax.ShapeDtypeStruct((m.own_left, rank), F32),
            jax.ShapeDtypeStruct((m.own_right, rank), F32),
        ),
        in_specs=[vmem] * 5,
        out_specs=(vmem, vmem),
        scratch_shapes=[
            pltpu.VMEM((n_expert, tokens), F32),
            pltpu.VMEM((n_expert, tokens), F32),
            pltpu.VMEM((m.rows, tokens), BF16),
            pltpu.VMEM((m.rows, tokens), F32),
            pltpu.VMEM((K, m.rows, m.wide), BF16),
            pltpu.VMEM((K, m.rows, m.wide), BF16),
            pltpu.VMEM((hidden, rank), BF16),
            pltpu.VMEM((m.rows, rank), BF16),
            pltpu.VMEM((m.rows, rank), BF16),
            pltpu.VMEM((m.rows, rank), BF16),
            pltpu.VMEM((K, m.wide, rank), F32),
            pltpu.VMEM((K, half, m.piece, rank), F32),
            pltpu.VMEM((K, half, m.piece, rank), F32),
            pltpu.VMEM((K, m.piece, rank), F32),
            pltpu.VMEM((K, m.wide, rank), BF16),
            pltpu.VMEM((rank, rank), F32),
            pltpu.VMEM((rank, rank), F32),
            pltpu.VMEM((m.rows, rank), F32),
            pltpu.VMEM((m.rows, rank), BF16),
            pltpu.VMEM((m.rows, rank), BF16),
            pltpu.VMEM((K, m.piece, rank), F32),
            pltpu.VMEM((hidden, rank), F32),
            pltpu.VMEM((hidden, rank), F32),
            pltpu.VMEM((8, rank), F32),
            pltpu.VMEM((8 * n_dp, rank), F32),
            dma((K,)),
            dma((K,)),
            dma((2,)),
            dma((2,)),
            dma((2,)),
            dma((2, K, half)),
            dma((2, K, half)),
            dma((2, K, half)),
            dma((2, K, half)),
            dma((2,)),
            dma((2, K)),
            dma((2,)),
            dma((2,)),
        ],
        compiler_params=pltpu.CompilerParams(
            collective_id=1, has_side_effects=True, vmem_limit_bytes=48 * 2**20
        ),
    )(
        cotangent, route_weights, token_experts,
        saved_hidden.reshape(m.rows, hidden), previous_right[0],
    )
    return (left[None], right[None])


def solution(mesh, chunks=5):
    in_specs = (
        P(("dp", "expert"), None),
        P(("dp", "expert"), None),
        P(("dp", "expert"), None),
        P("dp", "expert", None, None, None),
        P("expert", "dp", None),
    )
    out_specs = (P("expert", "dp", None), P("expert", "dp", None))
    return jax.shard_map(
        functools.partial(local, chunks), mesh=mesh, in_specs=in_specs, out_specs=out_specs, check_vma=False
    )
```

time: 625 us -> 303 us (0.48)
  the two profiles are of different devices: /device:TPU:32 before, /device:TPU:8 now
where the time goes in v1:
time: 303 us
  Pallas kernels  296 us (98%)
  local copies, waits for them, and re-layouts  6.33 us (2%)
    pallas_call x1, Pallas kernels, local(): pl.pallas_call(functools.partial(kernel, m), out_shape=(jax.ShapeDtypeStr...  296 us
    unnamed x10, local copies, waits for them, and re-layouts  6.33 us

profile of v1, /device:TPU:8, one launch (start us, length us, event | category | flops | bytes accessed | tf_op | source)
XLA Modules:
  0.0 302.6 jit_solution(12279377462186875998)
XLA Ops:
  0.6 0.8 copy.7.weights
  1.4 0.8 copy.8.experts
  2.2 0.0 copy-start
  2.2 1.4 copy-done
  3.6 0.0 copy-start.1
  3.6 1.3 copy-done.1
  4.9 0.0 copy-start.2
  4.9 0.7 copy-done.2
  5.7 295.7 %shard_map.68 = (f32[320,128]{1,0:T(8,128)S(1)}, f32[96,128]{1,0:T(8,128)S(1)}) custom-call(bf16[128,5120]{1,0:T(8,128)(2,1)S(1)} %copy-done.1, f32[128,6]{1,0:T(8,128)S(1)} %copy.7.weights, s32[128,6]{1,0:T(8,128)S(1)} %copy.8.experts, bf16[512,1536]{1,0:T(8,128)(2,1)S(1)} %bitcast.4, bf16[96,128]{1,0:T(8,128)(2,1)S(1)} %bitcast.7), custom_call_target="tpu_custom_call" | custom-call | tf_op jit(solution)/shard_map/pallas_call | solution.py:452
  301.4 0.7 copy.11
  302.0 0.6 copy.12
Async XLA Ops:
  2.2 1.4 copy-start
  3.6 1.3 copy-start.1
  4.9 0.7 copy-start.2
